TPU v7x, 32 devices: a whole 2x2x4 slice. The times are simulated.
32 devices in a mesh: groups: 2 (over y), space: 8 (over z, x), heads: 2 (over core).
Axes of the slice: x: 2, y: 2, z: 4, core: 2. Of those that a mesh axis runs over, the one named last changes fastest.
Arguments:
- queries: bfloat16 [2400, 1536], P(('groups', 'space'), 'heads'), parts along dimension 0, may hold values from -16 to 16
- latent_keys: bfloat16 [2400, 1536], P(('groups', 'space'), 'heads'), parts along dimension 0, may hold values from -9 to 9
- latent_values: bfloat16 [2400, 1536], P(('groups', 'space'), 'heads'), parts along dimension 0, may hold values from -6 to 6
- prompt: bfloat16 [512, 3072], P('groups'), parts along dimension 0, may hold values from -44 to 44
- key_weight: bfloat16 [3072, 1536], P('space', 'heads'), may hold values from -0.15625 to 0.15625
- value_weight: bfloat16 [3072, 1536], P('space', 'heads'), may hold values from -0.15625 to 0.15625
- out_weight: bfloat16 [1536, 3072], P('heads', 'space'), may hold values from -0.21875 to 0.21875
- tile_owner: int32 [16], P('groups'), parts along dimension 0, may hold values from 0 to 7, as said below
Outputs:
- block_output: bfloat16 [2400, 3072], P(('groups', 'space'), 'heads'), parts along dimension 0
There are 2 independent parts, one for each index of `groups`. A program takes and returns all parts, laid end to end along the dimension named above; an argument that names none is the same for every part. Nothing has to cross between parts.
Inputs may be any that keep to these rules, and one draw needn't show every extreme that they name: `tile_owner`: tile t = i * 2 + j of the 4 x 2 grid is held by slot a * 2 + b, with a = (i + r) mod 4 or a = (3 - i + r) mod 4 for one r, and b = j or b = 1 - j; r and each of the two alternatives are the same for all tiles.
All inputs are finite; a program needn't handle non-finite values.
Results may differ from a plain program's by a relative error of at most 0.0081.
Values may be sent and summed in bfloat16 or wider, within the bound.
A program may use at most 64 MiB of HBM per device.

v0:
```python
import jax
import jax.numpy as jnp
from jax import lax
from jax.sharding import PartitionSpec as P

HD = 128
RT = 16
RH = 56
TILE = 5
rope_theta = 256.0
eps_norm = 1e-06
masked_score = -1e30


def shifted(value, axis, steps):
    count = lax.axis_size(axis)
    pairs = [(source, (source + steps) % count) for source in range(count)]
    return lax.ppermute(value, axis, pairs)


def rope_tables(frame_pos, height_pos, width_pos):
    pairs_time = jnp.arange(RT // 2, dtype=jnp.float32)
    pairs_space = jnp.arange(RH // 2, dtype=jnp.float32)
    freq_time = rope_theta ** (-2.0 * pairs_time / RT)
    freq_space = rope_theta ** (-2.0 * pairs_space / RH)
    angles = jnp.concatenate(
        [
            frame_pos[:, None] * freq_time[None, :],
            height_pos[:, None] * freq_space[None, :],
            width_pos[:, None] * freq_space[None, :],
        ],
        axis=1,
    )
    return (jnp.cos(angles), jnp.sin(angles))


def rotate(stacked, cosine, sine_table):
    row_count = stacked.shape[0]
    head_total = stacked.shape[1]
    paired = stacked.reshape(row_count, head_total, HD // 2, 2)
    even_part = paired[..., 0]
    odd_part = paired[..., 1]
    cos_rows = cosine[:, None, :]
    sin_rows = sine_table[:, None, :]
    turned = jnp.stack(
        [even_part * cos_rows - odd_part * sin_rows, even_part * sin_rows + odd_part * cos_rows],
        axis=-1,
    )
    return turned.reshape(row_count, head_total * HD)


def normalize_keys(summed, head_total):
    row_count = summed.shape[0]
    half_width = summed.shape[1] // 2
    key_part = summed[:, :half_width].reshape(row_count, head_total, HD)
    key_part = key_part * lax.rsqrt(
        jnp.mean(key_part * key_part, axis=-1, keepdims=True) + eps_norm
    )
    return jnp.concatenate(
        [key_part.reshape(row_count, half_width), summed[:, half_width:]], axis=1
    ).astype(jnp.bfloat16)


def body(
    queries, latent_keys, latent_values, prompt, key_weight, value_weight, out_weight, tile_owner
):
    spaces = lax.axis_size("space")
    device = lax.axis_index("space")
    grid_h = min(8, spaces // 2)
    grid_w = spaces // grid_h
    tok_rows = queries.shape[0]
    head_width = queries.shape[1]
    head_count = head_width // HD
    tile_total = tile_owner.shape[0]
    tile_index = jnp.arange(tile_total, dtype=jnp.int32)
    own_tile = jnp.sum(jnp.where(tile_owner == device, tile_index, 0))
    tile_row = own_tile // grid_w
    tile_col = own_tile % grid_w
    anchor_slot = tile_owner[0]
    right_slot = tile_owner[min(1, tile_total - 1)]
    lower_slot = tile_owner[min(grid_w, tile_total - 1)]
    col_sign = jnp.where(right_slot % grid_w - anchor_slot % grid_w == -1, -1, 1)
    row_sign = jnp.where((lower_slot // grid_w - anchor_slot // grid_w) % grid_h == 1, 1, -1)
    cell_index = jnp.arange(tok_rows, dtype=jnp.int32)
    frame_pos = (cell_index // (TILE * TILE)).astype(jnp.float32)
    height_pos = (tile_row * TILE + cell_index // TILE % TILE).astype(jnp.float32)
    width_pos = (tile_col * TILE + cell_index % TILE).astype(jnp.float32)
    cosine, sine_table = rope_tables(frame_pos, height_pos, width_pos)
    query_rot = rotate(
        queries.astype(jnp.float32).reshape(tok_rows, head_count, HD), cosine, sine_table
    ).astype(jnp.bfloat16)
    key_rot = rotate(
        latent_keys.astype(jnp.float32).reshape(tok_rows, head_count, HD), cosine, sine_table
    ).astype(jnp.bfloat16)
    width_rows = key_weight.shape[0]
    text_cols = lax.dynamic_slice_in_dim(prompt, device * width_rows, width_rows, 1)
    both_weights = jnp.concatenate([key_weight, value_weight], axis=1)
    partial_text = jnp.dot(text_cols, both_weights, preferred_element_type=jnp.float32)
    summed_text = lax.psum(partial_text, "space")
    text_kv = normalize_keys(summed_text, head_count)
    kv_own = jnp.concatenate([key_rot, latent_values], axis=1)
    blocks = []
    valid_parts = []
    for row_step in (-1, 0, 1):
        for col_step in (-1, 0, 1):
            if row_step == 0 and col_step == 0:
                fetched = kv_own
            else:
                fetched = shifted(kv_own, "space", -(row_step * grid_w + col_step))
            near_row = tile_row + row_sign * row_step
            near_col = tile_col + col_sign * col_step
            inside = (near_row >= 0) & (near_row < grid_h) & (near_col >= 0) & (near_col < grid_w)
            blocks.append(fetched)
            valid_parts.append(jnp.zeros((tok_rows,), jnp.int32) + inside.astype(jnp.int32))
    blocks.append(text_kv)
    valid_parts.append(jnp.ones((text_kv.shape[0],), jnp.int32))
    keys_all = jnp.concatenate(blocks, axis=0)
    key_valid = jnp.concatenate(valid_parts, axis=0)
    score_scale = HD ** (-0.5)
    head_outputs = []
    for head_index in range(head_count):
        head_start = head_index * HD
        query_slice = query_rot[:, head_start : head_start + HD]
        key_slice = keys_all[:, head_start : head_start + HD]
        value_slice = keys_all[:, head_width + head_start : head_width + head_start + HD]
        scores = (
            lax.dot_general(
                query_slice, key_slice, (((1,), (1,)), ((), ())), preferred_element_type=jnp.float32
            )
            * score_scale
        )
        scores = jnp.where(key_valid[None, :] > 0, scores, masked_score)
        top_score = jnp.max(scores, axis=-1, keepdims=True)
        exponent = jnp.exp(scores - top_score)
        weights = (exponent / jnp.sum(exponent, axis=-1, keepdims=True)).astype(jnp.bfloat16)
        head_outputs.append(
            jnp.dot(weights, value_slice, preferred_element_type=jnp.float32).astype(jnp.bfloat16)
        )
    attended = jnp.concatenate(head_outputs, axis=1)
    partial_out = jnp.dot(
        attended,
        lax.all_gather(out_weight, "space", axis=1, tiled=True),
        preferred_element_type=jnp.float32,
    )
    summed_out = lax.psum_scatter(
        partial_out.astype(jnp.bfloat16), "heads", scatter_dimension=1, tiled=True
    )
    return summed_out


def solution(mesh):
    in_specs = (
        P(("groups", "space"), "heads"),
        P(("groups", "space"), "heads"),
        P(("groups", "space"), "heads"),
        P("groups", None),
        P("space", "heads"),
        P("space", "heads"),
        P("heads", "space"),
        P("groups"),
    )
    out_specs = P(("groups", "space"), "heads")
    return jax.shard_map(body, mesh=mesh, in_specs=in_specs, out_specs=out_specs, check_vma=False)
```

profile of v0, /device:TPU:0, one launch (start us, length us, event | category | flops | bytes accessed | tf_op | source)
XLA Modules:
  0.0 252.2 jit_solution(18399292161967376809)
XLA Ops:
  6.6 1.4 copy-done
  7.9 3.0 %fusion.6 = f32[256,1536]{1,0:T(8,128)} fusion(bf16[384,768]{1,0:T(8,128)(2,1)} %param.13, bf16[384,768]{1,0:T(8,128)(2,1)} %param.12, bf16[256,3072]{1,0:T(8,128)(2,1)S(1)} %copy-done, s32[]{:T(128)S(6)} %select_n.110), kind=kOutput, calls=%fused_computation.13 | convolution fusion | flops 304349184 | bytes 2949124 | tf_op jit(solution)/shard_map/dot_general | solution.py:98
  10.9 0.0 all-reduce.2.cloned.1.call-update
  10.9 0.0 all-gather.2.cloned.1.call-start
  11.0 0.7 all-gather.2.cloned.1.call-update
  11.7 0.0 reduce-scatter.2.cloned.1.call-start
  11.7 0.6 fusion.51
  15.0 0.2 copy.9
  15.2 0.5 reshape.201
  15.7 2.0 copy.10
  17.7 1.6 reshape.202
  19.3 0.1 broadcast_multiply_fusion.2
  19.4 0.1 broadcast_multiply_fusion.1
  19.5 0.2 fusion.42
  19.7 2.7 %subtract_convert_fusion.1 = (bf16[150,6,64,1]{0,3,2,1:T(2,128)(2,1)S(1)}, bf16[150,6,64,1]{0,3,2,1:T(2,128)(2,1)}, bf16[150,6,64,1]{0,3,2,1:T(2,128)(2,1)S(1)}, bf16[150,6,64,1]{0,3,2,1:T(2,128)(2,1)S(1)}) fusion(f32[150,6,64,2]{0,3,2,1:T(2,128)S(1)} %reshape.201, f32[150,64]{0,1:T(8,128)S(1)} %get-tuple-element.12, f32[150,64]{0,1:T(8,128)S(1)} %get-tuple-element.11, ...), kind=kLoop, calls=%fused_computation.69 | loop fusion | flops 921600 | bytes 1459200 | tf_op jit(solution)/shard_map/convert.7
  22.5 1.0 pad_maximum_fusion.3
  23.4 0.4 convert_element_type.111
  23.8 0.1 copy.11
  24.0 1.7 pad_maximum_fusion.1
  25.7 4.0 %collective-permute-start = (bf16[150,1536]{1,0:T(8,128)(2,1)}, bf16[150,1536]{1,0:T(8,128)(2,1)}, u32[]{:S(2)}, u32[]{:S(2)}) collective-permute-start(bf16[150,1536]{1,0:T(8,128)(2,1)} %pad_maximum_fusion.1), channel_id=1, source_target_pairs={{0,6},{2,8},{4,10},{6,12},{8,14},{10,0},{12,2},{14,4},{1,7},{3,9},... | collective-permute-start | bytes 1382408 | tf_op jit(solution)/shard_map/ppermute | solution.py:18
  29.7 1.6 collective-permute-start.1
  31.3 1.5 collective-permute-start.2
  32.8 3.2 %collective-permute-start.3 = (bf16[150,1536]{1,0:T(8,128)(2,1)}, bf16[150,1536]{1,0:T(8,128)(2,1)}, u32[]{:S(2)}, u32[]{:S(2)}) collective-permute-start(bf16[150,1536]{1,0:T(8,128)(2,1)} %pad_maximum_fusion.1), channel_id=1, source_target_pairs={{0,14},{2,0},{4,2},{6,4},{8,6},{10,8},{12,10},{14,12},{1,15},{3,1}... | collective-permute-start | bytes 1382408 | tf_op jit(solution)/shard_map/ppermute | solution.py:18
  36.0 0.5 collective-permute-start.4
  36.5 0.6 fusion.54
  43.3 2.0 pad_maximum_fusion.2
  45.3 1.1 convert_element_type.110
  46.5 0.1 concatenate.34
  46.6 91.5 %all-reduce.2.cloned.1.call-done = f32[256,1536]{1,0:T(8,128)} async-done(((f32[256,1536]{1,0:T(8,128)}), f32[256,1536]{1,0:T(8,128)}) %all-reduce.2.cloned.1.call-update) | async-done | bytes 1572880 | tf_op jit(solution)/shard_map/psum | solution.py:99
  138.1 1.2 slice_multiply_fusion
  139.3 0.3 copy.12
  139.6 0.1 reduce_sum.73
  139.6 0.1 mul.191
  139.7 0.3 copy.13
  140.0 1.2 slice.180
  141.1 0.0 collective-permute-done
  141.2 3.0 %collective-permute-start.5 = (bf16[150,1536]{1,0:T(8,128)(2,1)}, bf16[150,1536]{1,0:T(8,128)(2,1)S(1)}, u32[]{:S(2)}, u32[]{:S(2)}) collective-permute-start(bf16[150,1536]{1,0:T(8,128)(2,1)} %pad_maximum_fusion.1), channel_id=1, source_target_pairs={{0,10},{2,12},{4,14},{6,0},{8,2},{10,4},{12,6},{14,8},{1,11},{3,13... | collective-permute-start | bytes 1382408 | tf_op jit(solution)/shard_map/ppermute | solution.py:18
  144.1 1.2 multiply_convert_fusion
  145.3 0.1 pad_maximum_fusion
  145.4 0.0 collective-permute-done.1
  145.4 16.0 %collective-permute-done.5 = bf16[150,1536]{1,0:T(8,128)(2,1)S(1)} collective-permute-done((bf16[150,1536]{1,0:T(8,128)(2,1)}, bf16[150,1536]{1,0:T(8,128)(2,1)S(1)}, u32[]{:S(2)}, u32[]{:S(2)}) %collective-permute-start.5) | collective-permute-done | bytes 460832 | tf_op jit(solution)/shard_map/ppermute | solution.py:18
  161.5 34.4 %concatenate.39 = bf16[1606,1536]{1,0:T(8,128)(2,1)} concatenate(bf16[150,1536]{1,0:T(8,128)(2,1)} %collective-permute-done, bf16[150,1536]{1,0:T(8,128)(2,1)} %collective-permute-done.1, bf16[150,1536]{1,0:T(8,128)(2,1)} %collective-permute-done.2, bf16[150,1536]{1,0:T(8,128)(2,1)} %collective-permute-done.2, bf16[150,1536]{1,0:T(8,128)(2,1)} %pad_maximum_fusion.1, ...), dimensions={0} | concatenate | bytes 9867264 | tf_op jit(solution)/shard_map/concatenate | solution.py:117
  195.9 1.6 fusion.55
  197.5 0.3 fusion.16
  197.8 1.6 fusion.56
  199.4 0.3 fusion.17
  199.7 1.7 fusion.57
  201.4 0.3 fusion.18
  201.7 1.6 fusion.58
  203.3 0.3 fusion.19
  203.5 1.6 fusion.59
  205.1 0.3 fusion.20
  205.4 1.6 fusion.60
  207.0 0.3 fusion.21
  207.3 0.4 fusion.15
  207.7 0.4 fusion.14
  208.2 0.4 fusion.13
  208.6 0.4 fusion.12
  209.0 0.4 fusion.11
  209.4 0.4 fusion.10
  209.9 22.8 %all-gather.2.cloned.1.call-done = bf16[768,3072]{1,0:T(8,128)(2,1)} async-done(((bf16[768,384]{1,0:T(8,128)(2,1)}), bf16[768,3072]{1,0:T(8,128)(2,1)}) %all-gather.2.cloned.1.call-update) | async-done | bytes 4718608 | tf_op jit(solution)/shard_map/all_gather | solution.py:142
  232.6 4.2 %convolution_convert_fusion = bf16[150,3072]{1,0:T(8,128)(2,1)} fusion(bf16[150,768]{1,0:T(8,128)(2,1)S(1)} %fusion.10, bf16[768,3072]{1,0:T(8,128)(2,1)} %all-gather.2.cloned.1.call-done), kind=kOutput, calls=%fused_computation | convolution fusion | flops 708249600 | bytes 5870592 | tf_op jit(solution)/shard_map/dot_general | solution.py:140
  236.8 0.0 reduce-scatter.2.cloned.1.call-update
  236.8 8.8 %reduce-scatter.2.cloned.1.call-done = bf16[150,1536]{1,0:T(8,128)(2,1)} async-done(((bf16[150,3072]{1,0:T(8,128)(2,1)}), bf16[150,1536]{1,0:T(8,128)(2,1)}) %reduce-scatter.2.cloned.1.call-update) | async-done | bytes 460816 | tf_op jit(solution)/shard_map/reduce_scatter | solution.py:145
  (27 shorter events, 0.1 us)
Async XLA Ops:
  6.5 1.4 copy-start
  6.5 5.2 %copy-start.3 = (s32[8]{0:T(128)S(1)}, s32[8]{0:T(128)}, u32[]{:S(2)}) copy-start(s32[8]{0:T(128)} %param.15) | copy-start | bytes 100
  6.5 8.4 %copy-start.2 = (bf16[150,768]{1,0:T(8,128)(2,1)S(1)}, bf16[150,768]{1,0:T(8,128)(2,1)}, u32[]{:S(2)}) copy-start(bf16[150,768]{1,0:T(8,128)(2,1)} %param.8) | copy-start | bytes 691204
  6.5 131.5 %all-reduce.2.cloned.1.call-start = ((), (), s32[]{:S(2)}) async-start(), calls=%async_computation.1 | async-start | bytes 3145728 | tf_op jit(solution)/shard_map/psum | solution.py:99
  10.9 221.7 %all-gather.2.cloned.1.call-start = ((), (), s32[]{:S(2)}) async-start(), calls=%async_computation.2 | async-start | bytes 5308416 | tf_op jit(solution)/shard_map/all_gather | solution.py:142
  11.7 234.0 %reduce-scatter.2.cloned.1.call-start = ((), (), s32[]{:S(2)}) async-start(), calls=%async_computation.3 | async-start | bytes 1400832 | tf_op jit(solution)/shard_map/reduce_scatter | solution.py:145
  25.7 115.4 %collective-permute-start = (bf16[150,1536]{1,0:T(8,128)(2,1)}, bf16[150,1536]{1,0:T(8,128)(2,1)}, u32[]{:S(2)}, u32[]{:S(2)}) collective-permute-start(bf16[150,1536]{1,0:T(8,128)(2,1)} %pad_maximum_fusion.1), channel_id=1, source_target_pairs={{0,6},{2,8},{4,10},{6,12},{8,14},{10,0},{12,2},{14,4},{1,7},{3,9},... | collective-permute-start | bytes 1382408 | tf_op jit(solution)/shard_map/ppermute | solution.py:18
  29.7 115.7 %collective-permute-start.1 = (bf16[150,1536]{1,0:T(8,128)(2,1)}, bf16[150,1536]{1,0:T(8,128)(2,1)}, u32[]{:S(2)}, u32[]{:S(2)}) collective-permute-start(bf16[150,1536]{1,0:T(8,128)(2,1)} %pad_maximum_fusion.1), channel_id=1, source_target_pairs={{0,4},{2,6},{4,8},{6,10},{8,12},{10,14},{12,0},{14,2},{1,5},{3,7},... | collective-permute-start | bytes 1382408 | tf_op jit(solution)/shard_map/ppermute | solution.py:18
  31.3 114.1 %collective-permute-start.2 = (bf16[150,1536]{1,0:T(8,128)(2,1)}, bf16[150,1536]{1,0:T(8,128)(2,1)}, u32[]{:S(2)}, u32[]{:S(2)}) collective-permute-start(bf16[150,1536]{1,0:T(8,128)(2,1)} %pad_maximum_fusion.1), channel_id=1, source_target_pairs={{0,2},{2,4},{4,6},{6,8},{8,10},{10,12},{12,14},{14,0},{1,3},{3,5},... | collective-permute-start | bytes 1382408 | tf_op jit(solution)/shard_map/ppermute | solution.py:18
  32.8 112.6 %collective-permute-start.3 = (bf16[150,1536]{1,0:T(8,128)(2,1)}, bf16[150,1536]{1,0:T(8,128)(2,1)}, u32[]{:S(2)}, u32[]{:S(2)}) collective-permute-start(bf16[150,1536]{1,0:T(8,128)(2,1)} %pad_maximum_fusion.1), channel_id=1, source_target_pairs={{0,14},{2,0},{4,2},{6,4},{8,6},{10,8},{12,10},{14,12},{1,15},{3,1}... | collective-permute-start | bytes 1382408 | tf_op jit(solution)/shard_map/ppermute | solution.py:18
  36.0 109.4 %collective-permute-start.4 = (bf16[150,1536]{1,0:T(8,128)(2,1)}, bf16[150,1536]{1,0:T(8,128)(2,1)}, u32[]{:S(2)}, u32[]{:S(2)}) collective-permute-start(bf16[150,1536]{1,0:T(8,128)(2,1)} %pad_maximum_fusion.1), channel_id=1, source_target_pairs={{0,12},{2,14},{4,0},{6,2},{8,4},{10,6},{12,8},{14,10},{1,13},{3,15... | collective-permute-start | bytes 1382408 | tf_op jit(solution)/shard_map/ppermute | solution.py:18
  141.2 20.3 %collective-permute-start.5 = (bf16[150,1536]{1,0:T(8,128)(2,1)}, bf16[150,1536]{1,0:T(8,128)(2,1)S(1)}, u32[]{:S(2)}, u32[]{:S(2)}) collective-permute-start(bf16[150,1536]{1,0:T(8,128)(2,1)} %pad_maximum_fusion.1), channel_id=1, source_target_pairs={{0,10},{2,12},{4,14},{6,0},{8,2},{10,4},{12,6},{14,8},{1,11},{3,13... | collective-permute-start | bytes 1382408 | tf_op jit(solution)/shard_map/ppermute | solution.py:18
  199.6 7.7 %copy-start.1 = (bf16[1606,1536]{1,0:T(8,128)(2,1)S(1)}, bf16[1606,1536]{1,0:T(8,128)(2,1)}, u32[]{:S(2)}) copy-start(bf16[1606,1536]{1,0:T(8,128)(2,1)} %concatenate.39) | copy-start | bytes 14800900
Sparse Core Ops, SparseCore 0:
  11.1 126.9 all-reduce.1
  140.1 92.4 all-gather.1
  237.0 8.6 reduce-scatter.1
where the time goes:
time: 254 us; the launch traced here: 252 us
  waiting for transfers between devices  140 us (55%)
  local copies, waits for them, and re-layouts  44.1 us (17%)
  between operations  22.3 us (9%)
  matrix products  19.3 us (8%)
  starting transfers between devices  13.8 us (5%)
  other arithmetic  12.8 us (5%)
    psum x1, waiting for transfers between devices, body(): summed_text = lax.psum(partial_text, 'space')  91.5 us
    concatenate x1, local copies, waits for them, and re-layouts, body(): keys_all = jnp.concatenate(blocks, axis=0)  34.4 us
    all_gather x1, waiting for transfers between devices, body(): lax.all_gather(out_weight, 'space', axis=1, tiled=True)  22.8 us
    ppermute x6, waiting for transfers between devices, shifted(): return lax.ppermute(value, axis, pairs)  16.1 us
    ppermute x6, starting transfers between devices, shifted(): return lax.ppermute(value, axis, pairs)  13.7 us
    dot_general x6, matrix products, body(): lax.dot_general(query_slice, key_slice, (((1,), (1,)), ((), ())), preferr...  9.63 us
    reduce_scatter x1, waiting for transfers between devices, body(): lax.psum_scatter(partial_out.astype(jnp.bfloat16), 'heads', scatter_dimen...  8.8 us
  transfers between devices with their start and end apart: 9, of which 4 were waited for; matrix products, arithmetic and copies ran while one was open for 27% of the time, Pallas kernels for 0%

commit v1 on v0

--- a/solution.py
+++ b/solution.py
@@ -96,7 +96,7 @@
     text_cols = lax.dynamic_slice_in_dim(prompt, device * width_rows, width_rows, 1)
     both_weights = jnp.concatenate([key_weight, value_weight], axis=1)
     partial_text = jnp.dot(text_cols, both_weights, preferred_element_type=jnp.float32)
-    summed_text = lax.psum(partial_text, "space")
+    summed_text = jnp.sum(lax.all_gather(partial_text, "space"), axis=0)
     text_kv = normalize_keys(summed_text, head_count)
     kv_own = jnp.concatenate([key_rot, latent_values], axis=1)
     blocks = []

time: 254 us -> 361 us (1.42)
  waiting for transfers between devices: 140 us -> 236 us
  other arithmetic: 12.8 us -> 19.9 us
  local copies, waits for them, and re-layouts: 44.1 us -> 48.9 us
    all_gather x0 -> x1, waiting for transfers between devices: none -> 193 us  [body(): summed_text = jnp.sum(lax.all_gather(partial_text, 'space'), axis=0)]
    psum x1 -> x0, waiting for transfers between devices: 91.5 us -> none  [body(): summed_text = lax.psum(partial_text, 'space')]
    all_gather x1, waiting for transfers between devices: 22.8 us -> 7.3 us  [body(): lax.all_gather(out_weight, 'space', axis=1, tiled=True)]
    ppermute x6, waiting for transfers between devices: 16.1 us -> 23 us  [shifted(): return lax.ppermute(value, axis, pairs)]
    reduce_sum x0 -> x1, other arithmetic: none -> 6.17 us  [body(): summed_text = jnp.sum(lax.all_gather(partial_text, 'space'), axis=0)]
  transfers between devices with their start and end apart: 9 -> 9, of which waited for: 4 -> 4; matrix products, arithmetic and copies ran while one was open for 27% -> 22% of each run, Pallas kernels for 0% -> 0%
where the time goes in v1:
time: 361 us; the launch traced here: 359 us
  waiting for transfers between devices  236 us (65%)
  local copies, waits for them, and re-layouts  48.9 us (14%)
  between operations  22.9 us (6%)
  other arithmetic  19.9 us (6%)
  matrix products  19.4 us (5%)
  starting transfers between devices  12.4 us (3%)
    all_gather x1, waiting for transfers between devices, body(): summed_text = jnp.sum(lax.all_gather(partial_text, 'space'), axis=0)  193 us
    concatenate x1, local copies, waits for them, and re-layouts, body(): keys_all = jnp.concatenate(blocks, axis=0)  36.2 us
    ppermute x6, waiting for transfers between devices, shifted(): return lax.ppermute(value, axis, pairs)  23 us
    ppermute x6, starting transfers between devices, shifted(): return lax.ppermute(value, axis, pairs)  12.3 us
    reduce_scatter x1, waiting for transfers between devices, body(): lax.psum_scatter(partial_out.astype(jnp.bfloat16), 'heads', scatter_dimen...  11.9 us
    dot_general x6, matrix products, body(): lax.dot_general(query_slice, key_slice, (((1,), (1,)), ((), ())), preferr...  9.65 us
    all_gather x1, waiting for transfers between devices, body(): lax.all_gather(out_weight, 'space', axis=1, tiled=True)  7.3 us
  transfers between devices with their start and end apart: 9, of which 4 were waited for; matrix products, arithmetic and copies ran while one was open for 22% of the time, Pallas kernels for 0%

profile of v1, /device:TPU:0, one launch (start us, length us, event | category | flops | bytes accessed | tf_op | source)
XLA Modules:
  0.0 359.2 jit_solution(8512620936046549972)
XLA Ops:
  6.5 0.0 all-gather.6.cloned.1.call-start
  6.6 1.4 copy-done
  7.9 3.0 fusion.6
  11.0 0.0 all-gather.6.cloned.1.call-update
  11.0 0.0 all-gather.4.cloned.1.call-start
  11.0 0.7 all-gather.4.cloned.1.call-update
  11.7 0.0 reduce-scatter.2.cloned.1.call-start
  11.8 0.6 fusion.51
  15.0 0.2 copy.12
  15.2 0.5 reshape.201
  15.7 1.1 copy.13
  16.8 1.6 reshape.202
  18.5 0.1 broadcast_multiply_fusion.2
  18.6 0.1 broadcast_multiply_fusion.1
  18.6 0.2 fusion.42
  18.9 2.8 subtract_convert_fusion.1
  21.7 1.0 pad_maximum_fusion.3
  22.6 0.4 convert_element_type.111
  23.0 0.1 copy.14
  23.2 1.8 pad_maximum_fusion.1
  24.9 4.0 %collective-permute-start = (bf16[150,1536]{1,0:T(8,128)(2,1)}, bf16[150,1536]{1,0:T(8,128)(2,1)}, u32[]{:S(2)}, u32[]{:S(2)}) collective-permute-start(bf16[150,1536]{1,0:T(8,128)(2,1)} %pad_maximum_fusion.1), channel_id=1, source_target_pairs={{0,6},{2,8},{4,10},{6,12},{8,14},{10,0},{12,2},{14,4},{1,7},{3,9},... | collective-permute-start | bytes 1382408 | tf_op jit(solution)/shard_map/ppermute | solution.py:18
  28.9 1.6 collective-permute-start.1
  30.5 1.5 collective-permute-start.2
  32.1 3.2 collective-permute-start.3
  35.2 0.4 collective-permute-start.4
  35.7 0.6 fusion.54
  43.2 2.0 pad_maximum_fusion.2
  45.2 1.1 convert_element_type.110
  46.4 0.1 concatenate.34
  46.5 192.8 %all-gather.6.cloned.1.call-done = f32[2048,1536]{1,0:T(8,128)} async-done(((f32[256,1536]{1,0:T(8,128)}), f32[2048,1536]{1,0:T(8,128)}) %all-gather.6.cloned.1.call-update) | async-done | bytes 12582928 | tf_op jit(solution)/shard_map/all_gather | solution.py:99
  239.3 6.2 %reduce_sum.82 = f32[256,1536]{1,0:T(8,128)S(1)} reduce(f32[8,256,1536]{2,1,0:T(8,128)} %bitcast.16, f32[]{:T(128)} %constant.117.clone.1), dimensions={0}, to_apply=%region_1.2 | reduce | flops 2752512 | bytes 14155780 | tf_op jit(solution)/shard_map/reduce_sum | solution.py:99
  245.5 0.9 slice_multiply_fusion
  246.4 2.4 copy.15
  248.8 1.2 reduce_sum.83
  250.0 1.0 mul.191
  251.0 2.3 copy.16
  253.3 0.0 collective-permute-done
  253.3 1.5 collective-permute-start.5
  254.8 1.2 multiply_convert_fusion
  256.0 0.1 pad_maximum_fusion
  256.1 23.0 %collective-permute-done.5 = bf16[150,1536]{1,0:T(8,128)(2,1)} collective-permute-done((bf16[150,1536]{1,0:T(8,128)(2,1)}, bf16[150,1536]{1,0:T(8,128)(2,1)}, u32[]{:S(2)}, u32[]{:S(2)}) %collective-permute-start.5) | collective-permute-done | bytes 460832 | tf_op jit(solution)/shard_map/ppermute | solution.py:18
  279.1 36.2 %concatenate.39 = bf16[1606,1536]{1,0:T(8,128)(2,1)} concatenate(bf16[150,1536]{1,0:T(8,128)(2,1)} %collective-permute-done, bf16[150,1536]{1,0:T(8,128)(2,1)} %collective-permute-done.1, bf16[150,1536]{1,0:T(8,128)(2,1)} %collective-permute-done.2, bf16[150,1536]{1,0:T(8,128)(2,1)} %collective-permute-done.2, bf16[150,1536]{1,0:T(8,128)(2,1)} %pad_maximum_fusion.1, ...), dimensions={0} | concatenate | bytes 9867264 | tf_op jit(solution)/shard_map/concatenate | solution.py:117
  315.3 1.7 fusion.55
  317.0 0.3 fusion.16
  317.3 1.6 fusion.56
  318.9 0.3 fusion.17
  319.2 1.6 fusion.57
  320.7 0.3 fusion.18
  321.0 1.6 fusion.58
  322.6 0.3 fusion.19
  322.9 1.6 fusion.59
  324.5 0.3 fusion.20
  324.8 1.6 fusion.60
  326.4 0.3 fusion.21
  326.7 0.4 fusion.15
  327.1 0.4 fusion.14
  327.6 0.4 fusion.13
  328.0 0.4 fusion.12
  328.4 0.4 fusion.11
  328.8 0.4 fusion.10
  329.3 7.3 %all-gather.4.cloned.1.call-done = bf16[768,3072]{1,0:T(8,128)(2,1)} async-done(((bf16[768,384]{1,0:T(8,128)(2,1)}), bf16[768,3072]{1,0:T(8,128)(2,1)}) %all-gather.4.cloned.1.call-update) | async-done | bytes 4718608 | tf_op jit(solution)/shard_map/all_gather | solution.py:142
  336.6 4.2 %convolution_convert_fusion = bf16[150,3072]{1,0:T(8,128)(2,1)} fusion(bf16[150,768]{1,0:T(8,128)(2,1)S(1)} %fusion.10, bf16[768,3072]{1,0:T(8,128)(2,1)} %all-gather.4.cloned.1.call-done), kind=kOutput, calls=%fused_computation | convolution fusion | flops 708249600 | bytes 5870592 | tf_op jit(solution)/shard_map/dot_general | solution.py:140
  340.8 0.0 reduce-scatter.2.cloned.1.call-update
  340.8 11.9 %reduce-scatter.2.cloned.1.call-done = bf16[150,1536]{1,0:T(8,128)(2,1)} async-done(((bf16[150,3072]{1,0:T(8,128)(2,1)}), bf16[150,1536]{1,0:T(8,128)(2,1)}) %reduce-scatter.2.cloned.1.call-update) | async-done | bytes 460816 | tf_op jit(solution)/shard_map/reduce_scatter | solution.py:145
  (33 shorter events, 0.2 us)
Async XLA Ops:
  6.5 1.4 copy-start
  6.5 5.2 %copy-start.3 = (s32[8]{0:T(128)S(1)}, s32[8]{0:T(128)}, u32[]{:S(2)}) copy-start(s32[8]{0:T(128)} %param.15) | copy-start | bytes 100
  6.5 8.5 %copy-start.1 = (bf16[150,768]{1,0:T(8,128)(2,1)S(1)}, bf16[150,768]{1,0:T(8,128)(2,1)}, u32[]{:S(2)}) copy-start(bf16[150,768]{1,0:T(8,128)(2,1)} %param.8) | copy-start | bytes 691204
  6.5 9.2 %copy-start.2 = (bf16[150,768]{1,0:T(8,128)(2,1)S(1)}, bf16[150,768]{1,0:T(8,128)(2,1)}, u32[]{:S(2)}) copy-start(bf16[150,768]{1,0:T(8,128)(2,1)} %param.9) | copy-start | bytes 691204
  6.5 232.7 %all-gather.6.cloned.1.call-start = ((), (), s32[]{:S(2)}) async-start(), calls=%async_computation.3 | async-start | bytes 14155776 | tf_op jit(solution)/shard_map/all_gather | solution.py:99
  11.0 325.6 %all-gather.4.cloned.1.call-start = ((), (), s32[]{:S(2)}) async-start(), calls=%async_computation.1 | async-start | bytes 5308416 | tf_op jit(solution)/shard_map/all_gather | solution.py:142
  11.7 341.0 %reduce-scatter.2.cloned.1.call-start = ((), (), s32[]{:S(2)}) async-start(), calls=%async_computation.2 | async-start | bytes 1400832 | tf_op jit(solution)/shard_map/reduce_scatter | solution.py:145
  24.9 228.4 %collective-permute-start = (bf16[150,1536]{1,0:T(8,128)(2,1)}, bf16[150,1536]{1,0:T(8,128)(2,1)}, u32[]{:S(2)}, u32[]{:S(2)}) collective-permute-start(bf16[150,1536]{1,0:T(8,128)(2,1)} %pad_maximum_fusion.1), channel_id=1, source_target_pairs={{0,6},{2,8},{4,10},{6,12},{8,14},{10,0},{12,2},{14,4},{1,7},{3,9},... | collective-permute-start | bytes 1382408 | tf_op jit(solution)/shard_map/ppermute | solution.py:18
  28.9 227.2 %collective-permute-start.1 = (bf16[150,1536]{1,0:T(8,128)(2,1)}, bf16[150,1536]{1,0:T(8,128)(2,1)}, u32[]{:S(2)}, u32[]{:S(2)}) collective-permute-start(bf16[150,1536]{1,0:T(8,128)(2,1)} %pad_maximum_fusion.1), channel_id=1, source_target_pairs={{0,4},{2,6},{4,8},{6,10},{8,12},{10,14},{12,0},{14,2},{1,5},{3,7},... | collective-permute-start | bytes 1382408 | tf_op jit(solution)/shard_map/ppermute | solution.py:18
  30.5 225.6 %collective-permute-start.2 = (bf16[150,1536]{1,0:T(8,128)(2,1)}, bf16[150,1536]{1,0:T(8,128)(2,1)}, u32[]{:S(2)}, u32[]{:S(2)}) collective-permute-start(bf16[150,1536]{1,0:T(8,128)(2,1)} %pad_maximum_fusion.1), channel_id=1, source_target_pairs={{0,2},{2,4},{4,6},{6,8},{8,10},{10,12},{12,14},{14,0},{1,3},{3,5},... | collective-permute-start | bytes 1382408 | tf_op jit(solution)/shard_map/ppermute | solution.py:18
  32.1 224.0 %collective-permute-start.3 = (bf16[150,1536]{1,0:T(8,128)(2,1)}, bf16[150,1536]{1,0:T(8,128)(2,1)}, u32[]{:S(2)}, u32[]{:S(2)}) collective-permute-start(bf16[150,1536]{1,0:T(8,128)(2,1)} %pad_maximum_fusion.1), channel_id=1, source_target_pairs={{0,14},{2,0},{4,2},{6,4},{8,6},{10,8},{12,10},{14,12},{1,15},{3,1}... | collective-permute-start | bytes 1382408 | tf_op jit(solution)/shard_map/ppermute | solution.py:18
  35.2 220.9 %collective-permute-start.4 = (bf16[150,1536]{1,0:T(8,128)(2,1)}, bf16[150,1536]{1,0:T(8,128)(2,1)}, u32[]{:S(2)}, u32[]{:S(2)}) collective-permute-start(bf16[150,1536]{1,0:T(8,128)(2,1)} %pad_maximum_fusion.1), channel_id=1, source_target_pairs={{0,12},{2,14},{4,0},{6,2},{8,4},{10,6},{12,8},{14,10},{1,13},{3,15... | collective-permute-start | bytes 1382408 | tf_op jit(solution)/shard_map/ppermute | solution.py:18
  253.3 25.8 %collective-permute-start.5 = (bf16[150,1536]{1,0:T(8,128)(2,1)}, bf16[150,1536]{1,0:T(8,128)(2,1)}, u32[]{:S(2)}, u32[]{:S(2)}) collective-permute-start(bf16[150,1536]{1,0:T(8,128)(2,1)} %pad_maximum_fusion.1), channel_id=1, source_target_pairs={{0,10},{2,12},{4,14},{6,0},{8,2},{10,4},{12,6},{14,8},{1,11},{3,13... | collective-permute-start | bytes 1382408 | tf_op jit(solution)/shard_map/ppermute | solution.py:18
  315.3 11.4 %slice-start = ((s8[4939776]{0:T(1024)(128)(4,1)}), s8[4194304]{0:T(1024)(128)(4,1)S(1)}, s32[]{:S(2)}) async-start(s8[4939776]{0:T(1024)(128)(4,1)} %bitcast.17), calls=%async_computation.4 | async-start | bytes 8388608
  320.7 6.0 %slice-start.1 = ((s8[4939776]{0:T(1024)(128)(4,1)}), s8[745472]{0:T(1024)(128)(4,1)S(1)}, s32[]{:S(2)}) async-start(s8[4939776]{0:T(1024)(128)(4,1)} %bitcast.17), calls=%async_computation.5 | async-start | bytes 1490944
Sparse Core Ops, SparseCore 0:
  11.1 228.1 all-gather.5
  241.3 95.2 all-gather.3
  340.9 11.7 reduce-scatter.1
